TPU v7x, 512 devices: a whole 4x8x8 slice. The times are simulated.
512 devices in a mesh: snap: 16 (over y_lo, x, core), space: 32 (over z, y_hi).
Axes of the slice: x: 4, y: 8 (y_hi: 4, y_lo: 2; y = y_hi * 2 + y_lo), z: 8, core: 2. Of those that a mesh axis runs over, the one named last changes fastest.
Arguments:
- snapshots: bfloat16 [32768, 2048], P('space', 'snap')
- cell_weight: float32 [32768], P('space'), may hold values from 0.2 to 2
- eigvec: bfloat16 [2048, 256], replicated, may hold values from -0.125 to 0.125
- time_index: int32 [2048], replicated, may hold values from 0 to 2047, each once
Outputs:
- gram: float32 [2048, 2048], P('space', 'snap')
- modes: float32 [256, 32768], P('snap', 'space')
Inputs may be any that keep to these rules, and one draw needn't show every extreme that they name: `time_index`: each value of 0 to 2047 appears exactly once.
All inputs are finite; a program needn't handle non-finite values.
Results may differ from a plain program's by a relative error of at most 0.00081.
Values may be sent and summed in bfloat16 or wider, within the bound.
No kernel may reach another device: no remote copies, remote signals or barrier semaphores. Data moves between devices by JAX's collectives and lax.ppermute only.
A program may use at most 64 MiB of HBM per device.

v0:
```python
import jax
import jax.numpy as jnp
from jax import lax
from jax.sharding import PartitionSpec as P


def contract_rows(left, right):
    return lax.dot_general(
        left, right, (((0,), (0,)), ((), ())), preferred_element_type=jnp.float32
    )


def reduce_gram(make_rows, share_rows):
    return lax.psum_scatter(
        make_rows(jnp.int32(0), lax.axis_size("space") * share_rows),
        "space",
        scatter_dimension=0,
        tiled=True,
    )


def body(snapshots, cell_weight, eigvec, time_index):
    row_count, block_size = snapshots.shape
    snap_count = lax.axis_size("snap")
    snapshot_total = block_size * snap_count
    gram_share = snapshot_total // lax.axis_size("space")
    scaling = 1.0 / (row_count * lax.axis_size("space"))
    weighted = (snapshots.astype(jnp.float32) * cell_weight[:, None]).astype(jnp.bfloat16)
    ordered = jnp.take(eigvec, time_index, axis=0)
    mode_part = None
    gathered = lax.all_gather(snapshots, "snap", axis=1, tiled=True)

    def gram_terms(offset, length):
        return contract_rows(gathered, weighted) * scaling

    gram = reduce_gram(gram_terms, gram_share)
    local_weights = lax.dynamic_slice_in_dim(
        ordered, lax.axis_index("snap") * block_size, block_size, 0
    )
    mode_part = lax.psum_scatter(
        lax.dot_general(
            local_weights, snapshots, (((0,), (1,)), ((), ())), preferred_element_type=jnp.float32
        ),
        "snap",
        scatter_dimension=0,
        tiled=True,
    )
    return (gram, mode_part)


def solution(mesh):
    in_specs = (P("space", "snap"), P("space"), P(), P())
    out_specs = (P("space", "snap"), P("snap", "space"))
    return jax.shard_map(body, mesh=mesh, in_specs=in_specs, out_specs=out_specs, check_vma=False)
```

profile of v0, /device:TPU:6, one launch (start us, length us, event | category | flops | bytes accessed | tf_op | source)
XLA Modules:
  0.0 370.8 jit_solution(7543757270800126859)
XLA Ops:
  7.2 0.0 copy-start
  7.2 0.0 all-gather.2.cloned.1.call-start
  7.2 0.7 all-gather.2.cloned.1.call-update
  7.9 0.0 reduce-scatter.5.cloned.1.call-start
  8.0 0.7 fusion.5
  8.7 0.0 copy-done
  8.7 0.0 copy-start.2
  8.7 0.0 copy-start.1
  8.7 0.0 copy-start.3
  8.7 7.5 %gather_fusion = bf16[2048,256]{1,0:T(8,128)(2,1)S(1)} fusion(bf16[2048,256]{1,0:T(8,128)(2,1)S(1)} %copy-done, s32[2048]{0:T(1024)S(1)} %fusion.5), kind=kCustom, calls=%fused_computation | custom fusion | bytes 2105344 | tf_op jit(solution)/shard_map/jit(_take)/gather | solution.py:29
  16.2 0.0 copy-done.2
  16.2 0.1 dynamic-slice
  16.3 0.0 copy-done.1
  16.3 1.4 fusion.2
  17.7 0.0 reduce-scatter.5.cloned.1.call-update
  17.7 0.0 reduce-scatter.7.cloned.1.call-start
  17.8 46.7 %all-gather.2.cloned.1.call-done = bf16[1024,2048]{1,0:T(8,128)(2,1)} async-done(((bf16[1024,128]{1,0:T(8,128)(2,1)}), bf16[1024,2048]{1,0:T(8,128)(2,1)}) %all-gather.2.cloned.1.call-update) | async-done | bytes 4194320 | tf_op jit(solution)/shard_map/all_gather | solution.py:31
  64.4 0.0 copy-done.3
  64.4 3.0 fusion
  67.5 1.3 copy.8
  68.8 0.0 reduce-scatter.7.cloned.1.call-update
  68.8 62.5 %reduce-scatter.5.cloned.1.call-done = f32[16,1024]{1,0:T(8,128)} async-done(((f32[256,1024]{1,0:T(8,128)}), f32[16,1024]{1,0:T(8,128)}) %reduce-scatter.5.cloned.1.call-update) | async-done | bytes 65552 | tf_op jit(solution)/shard_map/reduce_scatter | solution.py:40
  131.3 232.9 %reduce-scatter.7.cloned.1.call-done = f32[64,128]{1,0:T(8,128)} async-done(((f32[2048,128]{1,0:T(8,128)}), f32[64,128]{1,0:T(8,128)}) %reduce-scatter.7.cloned.1.call-update) | async-done | bytes 32784
  (1 shorter events, 0.0 us)
Async XLA Ops:
  7.2 1.5 copy-start
  7.2 57.3 %all-gather.2.cloned.1.call-start = ((), (), s32[]{:S(2)}) async-start(), calls=%async_computation.2 | async-start | bytes 4456448 | tf_op jit(solution)/shard_map/all_gather | solution.py:31
  7.9 123.4 %reduce-scatter.5.cloned.1.call-start = ((), (), s32[]{:S(2)}) async-start(), calls=%async_computation.3 | async-start | bytes 1114112 | tf_op jit(solution)/shard_map/reduce_scatter | solution.py:40
  8.7 7.5 %copy-start.2 = (s32[2048]{0:T(1024)S(1)}, s32[2048]{0:T(1024)}, u32[]{:S(2)}) copy-start(s32[2048]{0:T(1024)} %param.7) | copy-start | bytes 24580
  8.7 7.6 %copy-start.1 = (bf16[1024,128]{1,0:T(8,128)(2,1)S(1)}, bf16[1024,128]{1,0:T(8,128)(2,1)}, u32[]{:S(2)}) copy-start(bf16[1024,128]{1,0:T(8,128)(2,1)} %param.4) | copy-start | bytes 786436
  8.7 55.8 %copy-start.3 = (f32[1024]{0:T(1024)S(1)}, f32[1024]{0:T(1024)}, u32[]{:S(2)}) copy-start(f32[1024]{0:T(1024)} %param.5) | copy-start | bytes 12292
  17.7 346.5 %reduce-scatter.7.cloned.1.call-start = ((), (), s32[]{:S(2)}) async-start(), calls=%async_computation.4 | async-start | bytes 1081344
Sparse Core Ops, SparseCore 0:
  10.1 54.3 all-gather.1
  67.8 63.4 reduce-scatter.4
  136.9 227.2 reduce-scatter.6
where the time goes:
time: 371 us
  waiting for transfers between devices  343 us (92%)
  between operations  13.8 us (4%)
  local copies, waits for them, and re-layouts  8.91 us (2%)
  matrix products  4.38 us (1%)
    unnamed x4, waiting for transfers between devices  234 us
    reduce_scatter x1, waiting for transfers between devices, body(): lax.psum_scatter(lax.dot_general(local_weights, snapshots, (((0,), (1,)),...  62.5 us
    all_gather x1, waiting for transfers between devices, body(): gathered = lax.all_gather(snapshots, 'snap', axis=1, tiled=True)  46.7 us
    gather x1, local copies, waits for them, and re-layouts, body(): ordered = jnp.take(eigvec, time_index, axis=0)  7.5 us
  transfers between devices with their start and end apart: 3, of which 3 were waited for; matrix products, arithmetic and copies ran while one was open for 4% of the time, Pallas kernels for 0%

commit v1 on v0

--- a/solution.py
+++ b/solution.py
@@ -28,7 +28,9 @@
     weighted = (snapshots.astype(jnp.float32) * cell_weight[:, None]).astype(jnp.bfloat16)
     ordered = jnp.take(eigvec, time_index, axis=0)
     mode_part = None
-    gathered = lax.all_gather(snapshots, "snap", axis=1, tiled=True)
+    gathered = jnp.concatenate(
+        lax.all_to_all(jnp.stack([snapshots] * lax.axis_size("snap")), "snap", 0, 0), axis=1
+    )
 
     def gram_terms(offset, length):
         return contract_rows(gathered, weighted) * scaling

time: 371 us -> 351 us (0.946)
  waiting for transfers between devices: 343 us -> 308 us
  starting transfers between devices: 0.12 us -> 10.4 us
    all_to_all x0 -> x1, waiting for transfers between devices: none -> 56 us  [body(): lax.all_to_all(jnp.stack([snapshots] * lax.axis_size('snap')), 'snap', 0, 0)]
    all_gather x1 -> x0, waiting for transfers between devices: 46.7 us -> none  [body(): gathered = lax.all_gather(snapshots, 'snap', axis=1, tiled=True)]
    reduce_scatter x1, waiting for transfers between devices: 62.5 us -> 18.3 us  [body(): lax.psum_scatter(lax.dot_general(local_weights, snapshots, (((0,), (1,)),...]
    all_to_all x0 -> x1, starting transfers between devices: none -> 10.3 us  [body(): lax.all_to_all(jnp.stack([snapshots] * lax.axis_size('snap')), 'snap', 0, 0)]
    unnamed x4 -> x3, waiting for transfers between devices: 234 us -> 234 us
where the time goes in v1:
time: 351 us
  waiting for transfers between devices  308 us (88%)
  between operations  14.1 us (4%)
  local copies, waits for them, and re-layouts  12.6 us (4%)
  starting transfers between devices  10.4 us (3%)
  matrix products  5.41 us (2%)
    unnamed x3, waiting for transfers between devices  234 us
    all_to_all x1, waiting for transfers between devices, body(): lax.all_to_all(jnp.stack([snapshots] * lax.axis_size('snap')), 'snap', 0, 0)  56 us
    reduce_scatter x1, waiting for transfers between devices, body(): lax.psum_scatter(lax.dot_general(local_weights, snapshots, (((0,), (1,)),...  18.3 us
    all_to_all x1, starting transfers between devices, body(): lax.all_to_all(jnp.stack([snapshots] * lax.axis_size('snap')), 'snap', 0, 0)  10.3 us
    gather x1, local copies, waits for them, and re-layouts, body(): ordered = jnp.take(eigvec, time_index, axis=0)  7.5 us
  transfers between devices with their start and end apart: 3, of which 3 were waited for; matrix products, arithmetic and copies ran while one was open for 4% of the time, Pallas kernels for 0%

profile of v1, /device:TPU:6, one launch (start us, length us, event | category | flops | bytes accessed | tf_op | source)
XLA Modules:
  0.0 350.6 jit_solution(18428438825407512486)
XLA Ops:
  7.2 0.0 copy-start
  7.2 1.2 copy.9
  8.4 2.5 stack.2
  10.9 0.0 copy-start.2
  10.9 10.3 %all-to-all-start = ((bf16[16,1024,128]{1,2,0:T(8,128)(2,1)}), bf16[16,1024,128]{1,2,0:T(8,128)(2,1)}, u32[]{:S(2)}, u32[]{:S(2)}) async-start(bf16[16,1024,128]{1,2,0:T(8,128)(2,1)} %stack.2), calls=%async_computation | async-start | bytes 8388608 | tf_op jit(solution)/shard_map/all_to_all | solution.py:32
  21.2 0.0 reduce-scatter.5.cloned.1.call-start
  21.2 0.0 copy-done.2
  21.2 0.0 copy-done
  21.2 0.0 copy-start.1
  21.2 0.0 copy-start.3
  21.3 7.5 %gather_fusion = bf16[2048,256]{1,0:T(8,128)(2,1)S(1)} fusion(bf16[2048,256]{1,0:T(8,128)(2,1)S(1)} %copy-done, s32[2048]{0:T(1024)S(1)} %fusion.5), kind=kCustom, calls=%fused_computation | custom fusion | bytes 2105344 | tf_op jit(solution)/shard_map/jit(_take)/gather | solution.py:29
  28.8 0.1 dynamic-slice
  28.9 0.0 copy-done.1
  28.9 1.4 fusion.2
  30.3 0.0 reduce-scatter.5.cloned.1.call-update
  30.3 0.0 reduce-scatter.7.cloned.1.call-start
  30.4 56.0 %all-to-all-done = bf16[16,1024,128]{1,2,0:T(8,128)(2,1)} async-done(((bf16[16,1024,128]{1,2,0:T(8,128)(2,1)}), bf16[16,1024,128]{1,2,0:T(8,128)(2,1)}, u32[]{:S(2)}, u32[]{:S(2)}) %all-to-all-start) | async-done | bytes 4194336 | tf_op jit(solution)/shard_map/all_to_all | solution.py:32
  86.4 0.0 copy-done.3
  86.4 4.0 %fusion = f32[2048,128]{0,1:T(8,128)S(1)} fusion(bf16[1024,2048]{0,1:T(8,128)(2,1)} %bitcast.1, bf16[1024,128]{1,0:T(8,128)(2,1)S(1)} %copy-done.1, f32[1024]{0:T(1024)S(1)} %copy-done.3), kind=kOutput, calls=%fused_computation.2 | convolution fusion | flops 537526272 | bytes 5509120 | tf_op jit(solution)/shard_map/dot_general | solution.py:8
  90.4 1.3 copy.11
  91.7 0.0 reduce-scatter.7.cloned.1.call-update
  91.7 18.3 %reduce-scatter.5.cloned.1.call-done = f32[16,1024]{1,0:T(8,128)} async-done(((f32[256,1024]{1,0:T(8,128)}), f32[16,1024]{1,0:T(8,128)}) %reduce-scatter.5.cloned.1.call-update) | async-done | bytes 65552 | tf_op jit(solution)/shard_map/reduce_scatter | solution.py:42
  110.0 233.8 %reduce-scatter.7.cloned.1.call-done = f32[64,128]{1,0:T(8,128)} async-done(((f32[2048,128]{1,0:T(8,128)}), f32[64,128]{1,0:T(8,128)}) %reduce-scatter.7.cloned.1.call-update) | async-done | bytes 32784
  (2 shorter events, 0.0 us)
Async XLA Ops:
  7.2 14.1 %copy-start = (bf16[2048,256]{1,0:T(8,128)(2,1)S(1)}, bf16[2048,256]{1,0:T(8,128)(2,1)}, u32[]{:S(2)}) copy-start(bf16[2048,256]{1,0:T(8,128)(2,1)} %param.6) | copy-start | bytes 3145732
  10.9 10.3 %copy-start.2 = (s32[2048]{0:T(1024)S(1)}, s32[2048]{0:T(1024)}, u32[]{:S(2)}) copy-start(s32[2048]{0:T(1024)} %param.7) | copy-start | bytes 24580
  10.9 75.5 %all-to-all-start = ((bf16[16,1024,128]{1,2,0:T(8,128)(2,1)}), bf16[16,1024,128]{1,2,0:T(8,128)(2,1)}, u32[]{:S(2)}, u32[]{:S(2)}) async-start(bf16[16,1024,128]{1,2,0:T(8,128)(2,1)} %stack.2), calls=%async_computation | async-start | bytes 8388608 | tf_op jit(solution)/shard_map/all_to_all | solution.py:32
  21.2 88.9 %reduce-scatter.5.cloned.1.call-start = ((), (), s32[]{:S(2)}) async-start(), calls=%async_computation.3 | async-start | bytes 1114112 | tf_op jit(solution)/shard_map/reduce_scatter | solution.py:42
  21.2 7.6 %copy-start.1 = (bf16[1024,128]{1,0:T(8,128)(2,1)S(1)}, bf16[1024,128]{1,0:T(8,128)(2,1)}, u32[]{:S(2)}) copy-start(bf16[1024,128]{1,0:T(8,128)(2,1)} %param.4) | copy-start | bytes 786436
  21.2 65.2 %copy-start.3 = (f32[1024]{0:T(1024)S(1)}, f32[1024]{0:T(1024)}, u32[]{:S(2)}) copy-start(f32[1024]{0:T(1024)} %param.5) | copy-start | bytes 12292
  30.3 313.5 %reduce-scatter.7.cloned.1.call-start = ((), (), s32[]{:S(2)}) async-start(), calls=%async_computation.4 | async-start | bytes 1081344
Sparse Core Ops, SparseCore 0:
  30.5 79.5 reduce-scatter.4
  115.6 228.1 reduce-scatter.6
